TPU v7x, 512 devices: a whole 4x4x16 slice. The times are simulated.
512 devices in a mesh: chan: 128 (over x, z, y_hi), tm: 4 (over y_lo, core).
Axes of the slice: x: 4, y: 4 (y_hi: 2, y_lo: 2; y = y_hi * 2 + y_lo), z: 16, core: 2. Of those that a mesh axis runs over, the one named last changes fastest.
Arguments:
- spectra: bfloat16 [256, 10240, 128], P('tm', 'chan'), may hold values from -150 to 150
- live_mask: int32 [10240], P('chan'), may hold values 0 or 1
Outputs:
- correlations: bfloat16 [2, 80, 10240, 128], P(None, 'tm', 'chan')
All inputs are finite; a program needn't handle non-finite values. No bound on the sum of `live_mask` on one device may be relied on, other than what follows from the above.
Results may differ from a plain program's by a relative error of at most 0.015.
Values may be sent and summed in bfloat16 or wider, within the bound.
A program may use at most 64 MiB of HBM per device.

v0:
```python
import math

import jax
import jax.numpy as jnp
from jax import lax
from jax.sharding import PartitionSpec as P

ROUNDS = 2


def from_behind(shard, axis, by):
    length = lax.axis_size(axis)
    return lax.ppermute(shard, axis, [(i, (i + by) % length) for i in range(length)])


def lag_table(frequency, windows_all):
    bins = jnp.arange(frequency).astype(jnp.float32)
    shifts = (jnp.arange(2 * frequency) - frequency).astype(jnp.float32)
    phase = 2.0 * math.pi / (2 * frequency) * bins[:, None] * shifts[None, :]
    weight = jnp.where(bins == 0, 1.0, 2.0).astype(jnp.float32)
    scaling = 1.0 / (2.0 * math.sqrt(frequency * windows_all))
    upper = weight[:, None] * jnp.cos(phase) * scaling
    lower = -weight[:, None] * jnp.sin(phase) * scaling
    return jnp.concatenate([upper, lower], axis=0)


def whiten(spectra, live_mask):
    values = spectra.astype(jnp.float32)
    mean_square = jnp.mean(values * values, axis=-1, keepdims=True)
    gated = values * live_mask.astype(jnp.float32)[None, :, None]
    return (gated * lax.rsqrt(mean_square + 1e-06)).astype(jnp.bfloat16)


def cross(own_block, other_block):
    half = own_block.shape[-1] // 2
    own_real, own_imag = (own_block[..., :half], own_block[..., half:])
    other_real, other_imag = (other_block[..., :half], other_block[..., half:])
    real_part = jnp.einsum("wjf,wif->jif", other_real, own_real, preferred_element_type=jnp.float32)
    real_part = real_part + jnp.einsum(
        "wjf,wif->jif", other_imag, own_imag, preferred_element_type=jnp.float32
    )
    imag_part = jnp.einsum("wjf,wif->jif", other_real, own_imag, preferred_element_type=jnp.float32)
    imag_part = imag_part - jnp.einsum(
        "wjf,wif->jif", other_imag, own_real, preferred_element_type=jnp.float32
    )
    return jnp.concatenate([real_part, imag_part], axis=-1)


def project(stacked, lag_matrix):
    width = stacked.shape[-1]
    lagged = jnp.dot(stacked.reshape(-1, width), lag_matrix, precision=lax.Precision.HIGHEST)
    return lagged.reshape(stacked.shape).astype(jnp.bfloat16)


def shards(spectra, live_mask):
    white = whiten(spectra, live_mask)
    frequency = spectra.shape[2] // 2
    lag_matrix = lag_table(frequency, spectra.shape[0] * lax.axis_size("tm"))
    share_rows = spectra.shape[1] // lax.axis_size("tm")
    partners = []
    for offset in range(1, ROUNDS + 1):
        partners.append(from_behind(white, "chan", -offset))
    results = []
    for partner in partners:

        def partial_term(first_row, row_count, partner=partner):
            return cross(white, partner)

        summed = lax.psum_scatter(
            partial_term(jnp.int32(0), share_rows * lax.axis_size("tm")).astype(jnp.bfloat16),
            "tm",
            scatter_dimension=0,
            tiled=True,
        ).astype(jnp.float32)
        results.append(project(summed, lag_matrix))
    return jnp.stack(results)


def solution(mesh):
    placed = (P("tm", "chan", None), P("chan"))
    return jax.shard_map(
        shards, mesh=mesh, in_specs=placed, out_specs=P(None, "tm", "chan", None), check_vma=False
    )
```

profile of v0, /device:TPU:1, one launch (start us, length us, event | category | flops | bytes accessed | tf_op | source)
XLA Modules:
  0.0 178.1 jit_solution(4050863009889182071)
XLA Ops:
  6.5 0.0 reduce-scatter.3.cloned.1.call-start
  6.5 2.5 %fusion.2 = f32[64,80]{1,0:T(8,128)S(1)} fusion(bf16[64,80,128]{2,1,0:T(8,128)(2,1)} %param.2), kind=kLoop, calls=%fused_computation.8 | loop fusion | flops 1960960 | bytes 1331200 | tf_op jit(solution)/shard_map/reduce_sum | solution.py:29
  9.0 0.7 convert_element_type.44
  9.7 2.0 %fusion.1 = bf16[64,80,128]{2,1,0:T(8,128)(2,1)S(1)} fusion(bf16[64,80,128]{2,1,0:T(8,128)(2,1)} %param.2, f32[64,80]{1,0:T(8,128)S(1)} %add_rsqrt_fusion, f32[80]{0:T(128)S(1)} %convert_element_type.44), kind=kLoop, calls=%fused_computation.7 | loop fusion | flops 2621440 | bytes 2642240 | tf_op jit(solution)/shard_map/convert_element_type | solution.py:31
  11.7 16.8 %collective-permute-start = (bf16[64,80,128]{2,1,0:T(8,128)(2,1)S(1)}, bf16[64,80,128]{2,1,0:T(8,128)(2,1)}, u32[]{:S(2)}, u32[]{:S(2)}) collective-permute-start(bf16[64,80,128]{2,1,0:T(8,128)(2,1)S(1)} %fusion.1), channel_id=1, source_target_pairs={{0,508},{4,0},{8,4},{12,8},{16,12},{20,16},{24,20},{28,24},{32,28}... | collective-permute-start | bytes 3932168 | tf_op jit(solution)/shard_map/ppermute | solution.py:13
  28.4 2.6 %collective-permute-start.1 = (bf16[64,80,128]{2,1,0:T(8,128)(2,1)S(1)}, bf16[64,80,128]{2,1,0:T(8,128)(2,1)}, u32[]{:S(2)}, u32[]{:S(2)}) collective-permute-start(bf16[64,80,128]{2,1,0:T(8,128)(2,1)S(1)} %fusion.1), channel_id=1, source_target_pairs={{0,504},{4,508},{8,0},{12,4},{16,8},{20,12},{24,16},{28,20},{32,24... | collective-permute-start | bytes 3932168 | tf_op jit(solution)/shard_map/ppermute | solution.py:13
  31.1 1.9 %fusion.18 = (bf16[64,80,64]{2,1,0:T(8,128)(2,1)}, bf16[64,80,64]{2,1,0:T(8,128)(2,1)}) fusion(bf16[64,80,128]{2,1,0:T(8,128)(2,1)S(1)} %fusion.1), kind=kLoop, calls=%fused_computation.36 | loop fusion | bytes 2621440 | tf_op jit(solution)/shard_map/slice | solution.py:36
  33.0 2.6 %copy.3 = bf16[64,80,64]{1,0,2:T(8,128)(2,1)S(1)} copy(bf16[64,80,64]{2,1,0:T(8,128)(2,1)} %get-tuple-element.9) | data formatting | bytes 1310720 | tf_op jit(solution)/shard_map/slice | solution.py:36
  35.7 2.6 %copy.6 = bf16[64,80,64]{1,0,2:T(8,128)(2,1)S(1)} copy(bf16[64,80,64]{2,1,0:T(8,128)(2,1)} %get-tuple-element.10) | data formatting | bytes 1310720 | tf_op jit(solution)/shard_map/slice | solution.py:36
  38.3 17.5 %collective-permute-done = bf16[64,80,128]{2,1,0:T(8,128)(2,1)} collective-permute-done((bf16[64,80,128]{2,1,0:T(8,128)(2,1)S(1)}, bf16[64,80,128]{2,1,0:T(8,128)(2,1)}, u32[]{:S(2)}, u32[]{:S(2)}) %collective-permute-start) | collective-permute-done | bytes 1310752 | tf_op jit(solution)/shard_map/ppermute | solution.py:13
  55.9 3.7 %fusion.16 = (bf16[64,80,64]{2,1,0:T(8,128)(2,1)}, bf16[64,80,64]{2,1,0:T(8,128)(2,1)}) fusion(bf16[64,80,128]{2,1,0:T(8,128)(2,1)} %collective-permute-done), kind=kLoop, calls=%fused_computation.34 | loop fusion | bytes 2621440 | tf_op jit(solution)/shard_map/slice | solution.py:37
  59.5 3.4 %copy.7 = bf16[64,80,64]{1,0,2:T(8,128)(2,1)} copy(bf16[64,80,64]{2,1,0:T(8,128)(2,1)} %get-tuple-element.5) | data formatting | bytes 1310720 | tf_op jit(solution)/shard_map/slice | solution.py:37
  62.9 3.3 %copy.4 = bf16[64,80,64]{1,0,2:T(8,128)(2,1)} copy(bf16[64,80,64]{2,1,0:T(8,128)(2,1)} %get-tuple-element.6) | data formatting | bytes 1310720 | tf_op jit(solution)/shard_map/slice | solution.py:37
  66.2 0.0 copy-start.3
  66.2 3.4 %fusion.22 = f32[64,80,80]{2,1,0:T(8,128)} fusion(bf16[64,80,64]{1,0,2:T(8,128)(2,1)S(1)} %copy.3, bf16[64,80,64]{1,0,2:T(8,128)(2,1)} %copy.7), kind=kOutput, calls=%fused_computation.40 | convolution fusion | flops 52428800 | bytes 2949120 | tf_op jit(solution)/shard_map/wjf,wif->jif/dot_general | solution.py:43
  69.6 0.0 copy-done.3
  69.6 0.0 copy-start.2
  69.6 2.1 %fusion.19 = f32[64,80,80]{2,1,0:T(8,128)} fusion(bf16[64,80,64]{1,0,2:T(8,128)(2,1)S(1)} %copy.3, bf16[64,80,64]{1,0,2:T(8,128)(2,1)S(1)} %copy-done.3), kind=kOutput, calls=%fused_computation.37 | convolution fusion | flops 52428800 | bytes 2949120 | tf_op jit(solution)/shard_map/wjf,wif->jif/dot_general | solution.py:38
  71.7 0.0 copy-done.2
  71.8 2.0 %fusion.20 = f32[64,80,80]{2,1,0:T(8,128)} fusion(bf16[64,80,64]{1,0,2:T(8,128)(2,1)S(1)} %copy.6, bf16[64,80,64]{1,0,2:T(8,128)(2,1)S(1)} %copy-done.2), kind=kOutput, calls=%fused_computation.38 | convolution fusion | flops 52428800 | bytes 2949120 | tf_op jit(solution)/shard_map/wjf,wif->jif/dot_general | solution.py:39
  73.8 2.0 %fusion.21 = f32[64,80,80]{2,1,0:T(8,128)} fusion(bf16[64,80,64]{1,0,2:T(8,128)(2,1)S(1)} %copy.6, bf16[64,80,64]{1,0,2:T(8,128)(2,1)S(1)} %copy-done.3), kind=kOutput, calls=%fused_computation.39 | convolution fusion | flops 52428800 | bytes 2949120 | tf_op jit(solution)/shard_map/wjf,wif->jif/dot_general | solution.py:42
  75.8 3.6 %copy.10 = f32[64,80,80]{0,1,2:T(8,128)} copy(f32[64,80,80]{2,1,0:T(8,128)} %fusion.22) | data formatting | bytes 3276800 | tf_op jit(solution)/shard_map/wjf,wif->jif/dot_general | solution.py:43
  79.4 3.7 %copy.5 = f32[64,80,80]{0,1,2:T(8,128)} copy(f32[64,80,80]{2,1,0:T(8,128)} %fusion.19) | data formatting | bytes 3276800 | tf_op jit(solution)/shard_map/wjf,wif->jif/dot_general | solution.py:38
  83.1 3.6 %copy.8 = f32[64,80,80]{0,1,2:T(8,128)} copy(f32[64,80,80]{2,1,0:T(8,128)} %fusion.20) | data formatting | bytes 3276800 | tf_op jit(solution)/shard_map/wjf,wif->jif/dot_general | solution.py:39
  86.7 3.6 %copy.9 = f32[64,80,80]{0,1,2:T(8,128)} copy(f32[64,80,80]{2,1,0:T(8,128)} %fusion.21) | data formatting | bytes 3276800 | tf_op jit(solution)/shard_map/wjf,wif->jif/dot_general | solution.py:42
  90.3 5.6 %fusion.3 = (bf16[80,80,64]{2,1,0:T(8,128)(2,1)S(1)}, bf16[80,80,64]{2,1,0:T(8,128)(2,1)S(1)}) fusion(f32[64,80,80]{0,1,2:T(8,128)} %copy.5, f32[64,80,80]{0,1,2:T(8,128)} %copy.8, f32[64,80,80]{0,1,2:T(8,128)} %copy.9, f32[64,80,80]{0,1,2:T(8,128)} %copy.10), kind=kLoop, calls=%fused_computation.9 | loop fusion | flops 1638400 | bytes 8192000 | tf_op jit(solution)/shard_map/add | solution.py:39
  95.9 2.0 %pad_maximum_fusion = bf16[80,80,128]{2,1,0:T(8,128)(2,1)} fusion(bf16[80,80,64]{2,1,0:T(8,128)(2,1)S(1)} %get-tuple-element.18, bf16[80,80,64]{2,1,0:T(8,128)(2,1)S(1)} %get-tuple-element.17), kind=kLoop, calls=%fused_computation.13 | loop fusion | flops 3276800 | bytes 3276800 | tf_op jit(solution)/shard_map/concatenate | solution.py:46
  98.0 0.0 reduce-scatter.3.cloned.1.call-update
  98.0 0.2 reduce-scatter.5.cloned.1.call-start
  98.2 0.0 collective-permute-done.1
  98.2 3.8 %fusion.17 = (bf16[64,80,64]{2,1,0:T(8,128)(2,1)}, bf16[64,80,64]{2,1,0:T(8,128)(2,1)}) fusion(bf16[64,80,128]{2,1,0:T(8,128)(2,1)} %collective-permute-done.1), kind=kLoop, calls=%fused_computation.35 | loop fusion | bytes 2621440 | tf_op jit(solution)/shard_map/slice | solution.py:37
  102.1 2.6 %copy.13 = bf16[64,80,64]{1,0,2:T(8,128)(2,1)S(1)} copy(bf16[64,80,64]{2,1,0:T(8,128)(2,1)} %get-tuple-element.7) | data formatting | bytes 1310720 | tf_op jit(solution)/shard_map/slice | solution.py:37
  104.7 2.1 %fusion.24 = f32[64,80,80]{2,1,0:T(8,128)} fusion(bf16[64,80,64]{1,0,2:T(8,128)(2,1)S(1)} %copy.6, bf16[64,80,64]{1,0,2:T(8,128)(2,1)S(1)} %copy.13), kind=kOutput, calls=%fused_computation.42 | convolution fusion | flops 52428800 | bytes 2949120 | tf_op jit(solution)/shard_map/wjf,wif->jif/dot_general | solution.py:39
  106.8 3.6 %copy.14 = f32[64,80,80]{0,1,2:T(8,128)} copy(f32[64,80,80]{2,1,0:T(8,128)} %fusion.24) | data formatting | bytes 3276800 | tf_op jit(solution)/shard_map/wjf,wif->jif/dot_general | solution.py:39
  110.4 3.3 %copy.11 = bf16[64,80,64]{1,0,2:T(8,128)(2,1)} copy(bf16[64,80,64]{2,1,0:T(8,128)(2,1)} %get-tuple-element.8) | data formatting | bytes 1310720 | tf_op jit(solution)/shard_map/slice | solution.py:37
  113.7 3.3 %fusion.25 = f32[64,80,80]{2,1,0:T(8,128)} fusion(bf16[64,80,64]{1,0,2:T(8,128)(2,1)S(1)} %copy.6, bf16[64,80,64]{1,0,2:T(8,128)(2,1)} %copy.11), kind=kOutput, calls=%fused_computation.43 | convolution fusion | flops 52428800 | bytes 2949120 | tf_op jit(solution)/shard_map/wjf,wif->jif/dot_general | solution.py:42
  117.1 3.7 %copy.15 = f32[64,80,80]{0,1,2:T(8,128)} copy(f32[64,80,80]{2,1,0:T(8,128)} %fusion.25) | data formatting | bytes 3276800 | tf_op jit(solution)/shard_map/wjf,wif->jif/dot_general | solution.py:42
  120.7 2.0 %fusion.26 = f32[64,80,80]{2,1,0:T(8,128)} fusion(bf16[64,80,64]{1,0,2:T(8,128)(2,1)S(1)} %copy.3, bf16[64,80,64]{1,0,2:T(8,128)(2,1)S(1)} %copy.13), kind=kOutput, calls=%fused_computation.44 | convolution fusion | flops 52428800 | bytes 2949120 | tf_op jit(solution)/shard_map/wjf,wif->jif/dot_general | solution.py:43
  122.8 0.0 copy-start.1
  122.8 3.7 %copy.16 = f32[64,80,80]{0,1,2:T(8,128)} copy(f32[64,80,80]{2,1,0:T(8,128)} %fusion.26) | data formatting | bytes 3276800 | tf_op jit(solution)/shard_map/wjf,wif->jif/dot_general | solution.py:43
  126.5 0.0 copy-done.1
  126.5 2.0 %fusion.23 = f32[64,80,80]{2,1,0:T(8,128)} fusion(bf16[64,80,64]{1,0,2:T(8,128)(2,1)S(1)} %copy.3, bf16[64,80,64]{1,0,2:T(8,128)(2,1)S(1)} %copy-done.1), kind=kOutput, calls=%fused_computation.41 | convolution fusion | flops 52428800 | bytes 2949120 | tf_op jit(solution)/shard_map/wjf,wif->jif/dot_general | solution.py:38
  128.5 0.0 copy-start
  128.5 3.8 %copy.12 = f32[64,80,80]{0,1,2:T(8,128)} copy(f32[64,80,80]{2,1,0:T(8,128)} %fusion.23) | data formatting | bytes 3276800 | tf_op jit(solution)/shard_map/wjf,wif->jif/dot_general | solution.py:38
  132.3 0.0 copy-done
  132.3 4.7 %fusion.5 = (bf16[80,80,64]{2,1,0:T(8,128)(2,1)S(1)}, bf16[80,80,64]{2,1,0:T(8,128)(2,1)S(1)}) fusion(f32[64,80,80]{0,1,2:T(8,128)} %copy.12, f32[64,80,80]{0,1,2:T(8,128)S(1)} %copy-done, f32[64,80,80]{0,1,2:T(8,128)} %copy.15, f32[64,80,80]{0,1,2:T(8,128)} %copy.16), kind=kLoop, calls=%fused_computation.11 | loop fusion | flops 1638400 | bytes 8192000 | tf_op jit(solution)/shard_map/add | solution.py:39
  137.0 2.1 %pad_maximum_fusion.1 = bf16[80,80,128]{2,1,0:T(8,128)(2,1)} fusion(bf16[80,80,64]{2,1,0:T(8,128)(2,1)S(1)} %get-tuple-element.14, bf16[80,80,64]{2,1,0:T(8,128)(2,1)S(1)} %get-tuple-element.13), kind=kLoop, calls=%fused_computation.14 | loop fusion | flops 3276800 | bytes 3276800 | tf_op jit(solution)/shard_map/concatenate | solution.py:46
  139.1 0.0 reduce-scatter.5.cloned.1.call-update
  139.1 0.2 fusion.10
  139.3 0.0 reduce-scatter.3.cloned.1.call-done
  139.3 1.5 fusion.7
  140.8 28.0 %reduce-scatter.5.cloned.1.call-done = bf16[20,80,128]{2,1,0:T(8,128)(2,1)} async-done(((bf16[80,80,128]{2,1,0:T(8,128)(2,1)}), bf16[20,80,128]{2,1,0:T(8,128)(2,1)}) %reduce-scatter.5.cloned.1.call-update) | async-done | bytes 409616 | tf_op jit(solution)/shard_map/reduce_scatter | solution.py:69
  168.8 1.5 fusion.8
  170.3 1.0 pad_maximum_fusion.2
  (4 shorter events, 0.0 us)
Async XLA Ops:
  6.5 132.8 %reduce-scatter.3.cloned.1.call-start = ((), (), s32[]{:S(2)}) async-start(), calls=%async_computation.2 | async-start | bytes 2048000 | tf_op jit(solution)/shard_map/reduce_scatter | solution.py:69
  11.7 44.2 %collective-permute-start = (bf16[64,80,128]{2,1,0:T(8,128)(2,1)S(1)}, bf16[64,80,128]{2,1,0:T(8,128)(2,1)}, u32[]{:S(2)}, u32[]{:S(2)}) collective-permute-start(bf16[64,80,128]{2,1,0:T(8,128)(2,1)S(1)} %fusion.1), channel_id=1, source_target_pairs={{0,508},{4,0},{8,4},{12,8},{16,12},{20,16},{24,20},{28,24},{32,28}... | collective-permute-start | bytes 3932168 | tf_op jit(solution)/shard_map/ppermute | solution.py:13
  28.4 69.8 %collective-permute-start.1 = (bf16[64,80,128]{2,1,0:T(8,128)(2,1)S(1)}, bf16[64,80,128]{2,1,0:T(8,128)(2,1)}, u32[]{:S(2)}, u32[]{:S(2)}) collective-permute-start(bf16[64,80,128]{2,1,0:T(8,128)(2,1)S(1)} %fusion.1), channel_id=1, source_target_pairs={{0,504},{4,508},{8,0},{12,4},{16,8},{20,12},{24,16},{28,20},{32,24... | collective-permute-start | bytes 3932168 | tf_op jit(solution)/shard_map/ppermute | solution.py:13
  66.2 3.4 %copy-start.3 = (bf16[64,80,64]{1,0,2:T(8,128)(2,1)S(1)}, bf16[64,80,64]{1,0,2:T(8,128)(2,1)}, u32[]{:S(2)}) copy-start(bf16[64,80,64]{1,0,2:T(8,128)(2,1)} %copy.4) | copy-start | bytes 1966084
  69.6 2.1 %copy-start.2 = (bf16[64,80,64]{1,0,2:T(8,128)(2,1)S(1)}, bf16[64,80,64]{1,0,2:T(8,128)(2,1)}, u32[]{:S(2)}) copy-start(bf16[64,80,64]{1,0,2:T(8,128)(2,1)} %copy.7) | copy-start | bytes 1966084
  98.0 70.8 %reduce-scatter.5.cloned.1.call-start = ((), (), s32[]{:S(2)}) async-start(), calls=%async_computation.3 | async-start | bytes 2048000 | tf_op jit(solution)/shard_map/reduce_scatter | solution.py:69
  122.8 3.7 %copy-start.1 = (bf16[64,80,64]{1,0,2:T(8,128)(2,1)S(1)}, bf16[64,80,64]{1,0,2:T(8,128)(2,1)}, u32[]{:S(2)}) copy-start(bf16[64,80,64]{1,0,2:T(8,128)(2,1)} %copy.11) | copy-start | bytes 1966084
  128.5 3.8 %copy-start = (f32[64,80,80]{0,1,2:T(8,128)S(1)}, f32[64,80,80]{0,1,2:T(8,128)}, u32[]{:S(2)}) copy-start(f32[64,80,80]{0,1,2:T(8,128)} %copy.14) | copy-start | bytes 4915204
Sparse Core Ops, SparseCore 0:
  98.1 29.5 reduce-scatter.2
  139.2 29.5 reduce-scatter.4
where the time goes:
time: 179 us; the launch traced here: 178 us
  local copies, waits for them, and re-layouts  56.6 us (32%)
  waiting for transfers between devices  45.6 us (25%)
  matrix products  22 us (12%)
  other arithmetic  20.7 us (12%)
  starting transfers between devices  19.6 us (11%)
  between operations  13.5 us (8%)
    reduce_scatter x2, waiting for transfers between devices, shards(): lax.psum_scatter(partial_term(jnp.int32(0), share_rows * lax.axis_size('t...  28 us
    slice x6, local copies, waits for them, and re-layouts, cross(): other_real, other_imag = (other_block[..., :half], other_block[..., half:])  20.2 us
    ppermute x2, starting transfers between devices, from_behind(): lax.ppermute(shard, axis, [(i, (i + by) % length) for i in range(length)])  19.4 us
    ppermute x2, waiting for transfers between devices, from_behind(): lax.ppermute(shard, axis, [(i, (i + by) % length) for i in range(length)])  17.5 us
    add x2, other arithmetic, cross(): real_part + jnp.einsum('wjf,wif->jif', other_imag, own_imag, preferred_el...  10.3 us
    dot_general x2, local copies, waits for them, and re-layouts, cross(): jnp.einsum('wjf,wif->jif', other_real, own_real, preferred_element_type=j...  7.43 us
    dot_general x2, local copies, waits for them, and re-layouts, cross(): jnp.einsum('wjf,wif->jif', other_imag, own_real, preferred_element_type=j...  7.31 us
    dot_general x2, local copies, waits for them, and re-layouts, cross(): jnp.einsum('wjf,wif->jif', other_real, own_imag, preferred_element_type=j...  7.3 us
  transfers between devices with their start and end apart: 4, of which 2 were waited for; matrix products, arithmetic and copies ran while one was open for 52% of the time, Pallas kernels for 0%

commit v1 on v0

v1 whole, which is shorter than its diff:
```python
import functools
import math

import jax
import jax.numpy as jnp
import ml_dtypes
import numpy as np
from jax import lax
from jax.experimental import pallas as pl
from jax.experimental.pallas import tpu as pltpu
from jax.sharding import PartitionSpec as P

MESH = pl.DeviceIdType.MESH
F32, BF16 = jnp.float32, jnp.bfloat16
PLANES = 64
SLOTS = 8
CH = 80
WIN = 64
LANES = 128
GROUPS = 4
ROWS = 112
DOWN, UP = 0, 1
DIRECTION = (DOWN, DOWN, DOWN, DOWN)


def lag_tables(windows_all):
    bins = np.arange(64)
    shifts = np.arange(128) - 64
    phase = 2.0 * np.pi / 128 * bins[:, None] * shifts[None, :]
    weight = np.where(bins == 0, 1.0, 2.0)
    scaling = 1.0 / (2.0 * math.sqrt(64 * windows_all))
    parts = np.stack([weight[:, None] * np.cos(phase), -weight[:, None] * np.sin(phase)]) * scaling
    parts = parts.reshape(2, SLOTS, GROUPS, 2, LANES)
    main = parts.transpose(0, 3, 2, 1, 4).reshape(LANES, LANES)
    rest = parts.transpose(3, 0, 2, 1, 4).reshape(LANES, LANES)
    return np.stack([main, rest]).astype(ml_dtypes.bfloat16)


def flip(slot, bits):
    for bit in range(3):
        if bits >> bit & 1:
            step = 1 << bit
            slot = slot + step - 2 * step * ((slot // step) % 2)
    return slot


def device(plane, slot):
    plane = (plane + PLANES) % PLANES
    return (plane * 2 + slot // 4, slot % 4)


def kernel(x_ref, mask_ref, lag_ref, out_ref, xf, tf, sent, own, other, made, got, gotf,
           send_a, recv_a, send_z, recv_z, send_r, recv_r, local):
    plane = lax.axis_index("chan") // 2
    quarter = lax.axis_index("tm")
    slot = (lax.axis_index("chan") % 2) * 4 + quarter
    any_up = UP in DIRECTION

    barrier = pltpu.get_barrier_semaphore()
    greeted = [device(plane, flip(slot, k)) for k in range(1, SLOTS)]
    for step in (-1, 1):
        greeted += [device(plane + step, flip(slot, k)) for k in range(SLOTS if any_up else 1)]
    for target in greeted:
        pl.semaphore_signal(barrier, inc=1, device_id=target, device_id_type=MESH)

    lane = lax.broadcasted_iota(jnp.int32, (64, LANES), 1)
    low = lane < 64

    def widen(n, carry):
        rows = pl.ds(pl.multiple_of(n * 128, 128), 128)
        xf[rows, :] = x_ref[rows, :].astype(F32)
        return carry

    lax.fori_loop(0, WIN * CH // 128, widen, 0)

    def turn(channel, place):
        pair = [xf[pl.ds(channel + k, WIN, stride=CH), :] for k in range(2)]
        z = jnp.concatenate(pair, axis=0).T
        power = jnp.sum(z * z, axis=0, keepdims=True) * (1.0 / LANES)
        live0 = mask_ref[channel].astype(F32)
        live1 = mask_ref[channel + 1].astype(F32)
        z = z * (lax.rsqrt(power + 1e-6) * jnp.where(low[:1], live0, live1))
        top, bottom = z[:64], z[64:]
        tf[pl.ds(place, 64, stride=CH), :] = jnp.where(low, top, pltpu.roll(bottom, 64, 1))
        tf[pl.ds(place + 1, 64, stride=CH), :] = jnp.where(low, pltpu.roll(top, 64, 1), bottom)

    def turn_first(n, carry):
        turn(20 * (n // 8) + 2 * (n % 8), 2 * n)
        return carry

    def turn_rest(n, carry):
        turn(20 * (n // 2) + 16 + 2 * (n % 2), 64 + 2 * n)
        return carry

    lax.fori_loop(0, 32, turn_first, 0)
    lax.fori_loop(0, 8, turn_rest, 0)

    def exchange(g, k):
        peer = flip(slot, k)
        return pltpu.make_async_remote_copy(
            src_ref=sent.at[peer, g], dst_ref=own.at[g, slot],
            send_sem=send_a.at[g, k], recv_sem=recv_a.at[g, k],
            device_id=device(plane, peer), device_id_type=MESH)

    def keep(g):
        return pltpu.make_async_copy(sent.at[slot, g], own.at[g, slot], local.at[g])

    for g in range(GROUPS):
        def narrow(d, carry, g=g):
            for ff in range(2):
                row = pl.multiple_of((d * 8 + g * 2 + ff) * CH, 16)
                sent[d, g, ff] = tf[pl.ds(row, CH), :].astype(BF16)
            return carry

        lax.fori_loop(0, SLOTS, narrow, 0)
        if g == 0:
            pl.semaphore_wait(barrier, len(greeted))
        for k in (4, 5, 6, 7, 2, 3, 1):
            exchange(g, k).start()
        keep(g).start()

    def forward(g):
        step = -1 if DIRECTION[g] == DOWN else 1
        return pltpu.make_async_remote_copy(
            src_ref=own.at[g], dst_ref=other.at[g], send_sem=send_z.at[g], recv_sem=recv_z.at[g],
            device_id=device(plane + step, slot), device_id_type=MESH)

    for g in range(GROUPS):
        keep(g).wait()
        for k in range(1, SLOTS):
            exchange(g, k).wait_recv()
        forward(g).start()

    sign = jnp.where(low[:1], 1.0, -1.0).astype(F32)
    piece = lax.broadcasted_iota(jnp.int32, (CH, LANES), 1) // 32

    def block(ref, g, which, ff):
        return jnp.concatenate([ref[g, which * 4 + q, ff] for q in range(4)], axis=1)

    def crossed(ref, g, which, ff):
        parts = [pltpu.roll(ref[g, which * 4 + q, ff].astype(F32), 64, 1) * sign for q in range(4)]
        return jnp.concatenate(parts, axis=1).astype(BF16)

    def cross(g):
        lower, upper = (own, other) if DIRECTION[g] == DOWN else (other, own)
        for b in range(2):
            left, rest = [], []
            for ff in range(2):
                plain, turned = block(lower, g, b, ff), crossed(lower, g, b, ff)
                tail = [plain[64:], turned[64:]]
                weights = jnp.concatenate([plain[:64], turned[:64]] + tail * 4, axis=0)
                first = block(lower, g, 1, ff) if b == 0 else block(upper, g, 0, ff)
                second = block(upper, g, b, ff)
                streamed = jnp.concatenate([first, second], axis=0)
                product = lax.dot_general(streamed, weights, (((1,), (1,)), ((), ())),
                                          preferred_element_type=F32)
                for r in range(2):
                    part = product[r * CH:(r + 1) * CH]
                    for t in range(4):
                        made[g, b * 4 + t, pl.ds(ff * 32 + r * 16, 16), :] = (
                            part[t * 16:(t + 1) * 16, :LANES].astype(BF16))
                    left.append(part[64:, :LANES])
                    rest.append(part[:, LANES:])
            edge = jnp.where(piece < 2, jnp.where(piece < 1, rest[0], rest[1]),
                             jnp.where(piece < 3, rest[2], rest[3])).astype(BF16)
            for t in range(4):
                fours = jnp.concatenate([a[t * 4:(t + 1) * 4] for a in left], axis=0)
                made[g, b * 4 + t, pl.ds(64, 16), :] = fours.astype(BF16)
                made[g, b * 4 + t, pl.ds(80, 16), :] = edge[t * 16:(t + 1) * 16]
                made[g, b * 4 + t, pl.ds(96, 16), :] = edge[64:]

    def deliver(g, k):
        owner = flip(slot, k)
        step = 0 if DIRECTION[g] == DOWN else -1
        return pltpu.make_async_remote_copy(
            src_ref=made.at[g, owner], dst_ref=got.at[g, slot],
            send_sem=send_r.at[g, k], recv_sem=recv_r.at[g, k],
            device_id=device(plane + step, owner), device_id_type=MESH)

    def retain(g):
        return pltpu.make_async_copy(made.at[g, slot], got.at[g, slot], local.at[GROUPS + g])

    for g in range(GROUPS):
        forward(g).wait_recv()
        cross(g)
        if DIRECTION[g] == DOWN:
            retain(g).start()
        for k in (4, 5, 6, 7, 2, 3, 1) + ((0,) if DIRECTION[g] == UP else ()):
            deliver(g, k).start()

    for g in range(GROUPS):
        if DIRECTION[g] == DOWN:
            retain(g).wait()
        for k in range(0 if DIRECTION[g] == UP else 1, SLOTS):
            deliver(g, k).wait_recv()

        def spread(d, carry, g=g):
            row = pl.multiple_of((g * SLOTS + d) * ROWS, 16)
            gotf[pl.ds(row, ROWS), :] = got[g, d].astype(F32)
            return carry

        lax.fori_loop(0, SLOTS, spread, 0)

    sources = GROUPS * SLOTS
    low16 = lax.broadcasted_iota(jnp.int32, (16, LANES), 1) // 32

    def rows_of(row):
        return gotf[pl.ds(row, sources, stride=ROWS), :]

    def lags(first, row_main, row_edge, stride_ff, stride_r):
        z = jnp.concatenate([rows_of(row_edge + j) for j in range(4)], axis=0).T
        pieces = []
        for j in range(4):
            for r in range(2):
                total = None
                for ff in range(2):
                    for c in range(2):
                        at = (ff * 4 + r * 2 + c) * 16
                        to = ff * 2 + c
                        moved = z[at:at + 16]
                        if (to - j) % 4:
                            moved = pltpu.roll(moved, ((to - j) % 4) * 32, 1)
                        total = moved if total is None else jnp.where(low16 == to, moved, total)
                pieces.append(total)
        edge = jnp.dot(jnp.concatenate(pieces, axis=0).astype(BF16), lag_ref[1], preferred_element_type=F32)
        for r in range(2):
            for half in range(2):
                rows = []
                for j in (2 * half, 2 * half + 1):
                    for ff in range(2):
                        rows.append(rows_of(row_main + ff * stride_ff + r * stride_r + j))
                z = jnp.concatenate(rows, axis=0).T
                top, bottom = z[:64], z[64:]
                lhs = jnp.concatenate([jnp.where(low, top, pltpu.roll(bottom, 64, 1)),
                                       jnp.where(low, pltpu.roll(top, 64, 1), bottom)], axis=0)
                body = jnp.dot(lhs.astype(BF16), lag_ref[0], preferred_element_type=F32)
                for n in range(2):
                    j = 2 * half + n
                    at = (j * 2 + r) * 16
                    pieces = []
                    for t in range(4):
                        pieces.append(body[n * 64 + t * 16:n * 64 + (t + 1) * 16])
                        pieces.append(edge[at + t * 4:at + (t + 1) * 4])
                    out_ref[r, first + j] = jnp.concatenate(pieces, axis=0).astype(BF16)

    def lags_first(n, carry):
        lags(4 * n, 4 * n, 80 + 4 * n, 32, 16)
        return carry

    lax.fori_loop(0, 4, lags_first, 0)
    lags(16, 64, 96 + 4 * quarter, 8, 4)

    for g in range(GROUPS):
        for k in range(1, SLOTS):
            exchange(g, k).wait_send()
        forward(g).wait_send()
        for k in range(0 if DIRECTION[g] == UP else 1, SLOTS):
            deliver(g, k).wait_send()


def shards(spectra, live_mask):
    windows = spectra.shape[0] * lax.axis_size("tm")
    tables = jnp.asarray(lag_tables(windows))
    vmem = pl.BlockSpec(memory_space=pltpu.VMEM)
    dma = pltpu.SemaphoreType.DMA
    return pl.pallas_call(
        kernel,
        out_shape=jax.ShapeDtypeStruct((2, 20, CH, LANES), BF16),
        in_specs=[vmem, pl.BlockSpec(memory_space=pltpu.SMEM), vmem],
        out_specs=vmem,
        scratch_shapes=[
            pltpu.VMEM((WIN * CH, LANES), F32),
            pltpu.VMEM((64 * CH, LANES), F32),
            pltpu.VMEM((SLOTS, GROUPS, 2, CH, LANES), BF16),
            pltpu.VMEM((GROUPS, SLOTS, 2, CH, LANES), BF16),
            pltpu.VMEM((GROUPS, SLOTS, 2, CH, LANES), BF16),
            pltpu.VMEM((GROUPS, SLOTS, ROWS, LANES), BF16),
            pltpu.VMEM((GROUPS, SLOTS, ROWS, LANES), BF16),
            pltpu.VMEM((GROUPS * SLOTS * ROWS, LANES), F32),
            dma((GROUPS, SLOTS)), dma((GROUPS, SLOTS)),
            dma((GROUPS,)), dma((GROUPS,)),
            dma((GROUPS, SLOTS)), dma((GROUPS, SLOTS)),
            dma((2 * GROUPS,)),
        ],
        compiler_params=pltpu.CompilerParams(
            collective_id=0, has_side_effects=True, vmem_limit_bytes=40 * 2**20),
        name="correlate",
    )(spectra.reshape(WIN * CH, LANES), live_mask, tables)


def solution(mesh):
    placed = (P("tm", "chan", None), P("chan"))
    return jax.shard_map(
        shards, mesh=mesh, in_specs=placed, out_specs=P(None, "tm", "chan", None), check_vma=False
    )
```

time: 179 us -> 63 us (0.35)
  Pallas kernels: 0 us -> 58.7 us
  local copies, waits for them, and re-layouts: 56.6 us -> 3.7 us
  waiting for transfers between devices: 45.6 us -> 0 us
  matrix products: 22 us -> 0 us
  other arithmetic: 20.7 us -> 0 us
  starting transfers between devices: 19.6 us -> 0 us
  between operations: 13.5 us -> 0.01 us
    pallas_call x0 -> x1, Pallas kernels: none -> 58.7 us  [shards(): pl.pallas_call(kernel, out_shape=jax.ShapeDtypeStruct((2, 20, CH, LANES),...]
    dot_general x8 -> x0, local copies, waits for them, and re-layouts: 29.3 us -> none  [the longest x2 7.43 us: cross(): jnp.einsum('wjf,wif->jif', other_real, own_real, preferred_element_type=j...]
    reduce_scatter x2 -> x0, waiting for transfers between devices: 28 us -> none  [shards(): lax.psum_scatter(partial_term(jnp.int32(0), share_rows * lax.axis_size('t...]
    slice x9 -> x0, local copies, waits for them, and re-layouts: 27.4 us -> none  [the longest x6 20.2 us: cross(): other_real, other_imag = (other_block[..., :half], other_block[..., half:])]
    dot_general x10 -> x0, matrix products: 22 us -> none  [the longest x2 5.44 us: cross(): jnp.einsum('wjf,wif->jif', other_imag, own_real, preferred_element_type=j...]
    ppermute x2 -> x0, starting transfers between devices: 19.4 us -> none  [from_behind(): lax.ppermute(shard, axis, [(i, (i + by) % length) for i in range(length)])]
    ppermute x2 -> x0, waiting for transfers between devices: 17.5 us -> none  [from_behind(): lax.ppermute(shard, axis, [(i, (i + by) % length) for i in range(length)])]
    add x2 -> x0, other arithmetic: 10.3 us -> none  [cross(): real_part + jnp.einsum('wjf,wif->jif', other_imag, own_imag, preferred_el...]
  transfers between devices with their start and end apart: 4 -> 0, of which waited for: 2 -> 0; matrix products, arithmetic and copies ran while one was open for 52% -> 0% of each run, Pallas kernels for 0% -> 0%
where the time goes in v1:
time: 63 us; the launch traced here: 62.4 us
  Pallas kernels  58.7 us (93%)
  local copies, waits for them, and re-layouts  3.7 us (6%)
    pallas_call x1, Pallas kernels, shards(): pl.pallas_call(kernel, out_shape=jax.ShapeDtypeStruct((2, 20, CH, LANES),...  58.7 us
    unnamed x7, local copies, waits for them, and re-layouts  3.7 us

profile of v1, /device:TPU:1, one launch (start us, length us, event | category | flops | bytes accessed | tf_op | source)
XLA Modules:
  0.0 62.4 jit_solution(7866153137383082707)
XLA Ops:
  0.0 0.0 copy-start
  0.0 1.3 %copy-done = bf16[64,80,128]{2,1,0:T(8,128)(2,1)S(1)} copy-done((bf16[64,80,128]{2,1,0:T(8,128)(2,1)S(1)}, bf16[64,80,128]{2,1,0:T(8,128)(2,1)}, u32[]{:S(2)}) %copy-start) | copy-done | bytes 1310744
  1.3 0.0 copy-start.1
  1.3 0.8 %copy-done.1 = bf16[2,128,128]{2,1,0:T(8,128)(2,1)S(1)} copy-done((bf16[2,128,128]{2,1,0:T(8,128)(2,1)S(1)}, bf16[2,128,128]{2,1,0:T(8,128)(2,1)}, u32[]{:S(2)}) %copy-start.1) | copy-done | bytes 65560
  2.2 0.0 copy-start.2
  2.2 0.7 %copy-done.2 = s32[80]{0:T(128)S(1)} copy-done((s32[80]{0:T(128)S(1)}, s32[80]{0:T(128)}, u32[]{:S(2)}) %copy-start.2) | copy-done | bytes 344
  2.8 58.7 %correlate.1 = bf16[2,20,80,128]{3,2,1,0:T(8,128)(2,1)S(1)} custom-call(bf16[5120,128]{1,0:T(8,128)(2,1)S(1)} %bitcast.1, s32[80]{0:T(128)S(1)} %copy-done.2, bf16[2,128,128]{2,1,0:T(8,128)(2,1)S(1)} %copy-done.1), custom_call_target="tpu_custom_call" | custom-call | tf_op jit(solution)/shard_map/correlate/pallas_call | solution.py:266
  61.5 0.9 %copy.5 = bf16[2,20,80,128]{3,2,1,0:T(8,128)(2,1)} copy(bf16[2,20,80,128]{3,2,1,0:T(8,128)(2,1)S(1)} %correlate.1) | data formatting | bytes 1638400
Async XLA Ops:
  0.0 1.3 %copy-start = (bf16[64,80,128]{2,1,0:T(8,128)(2,1)S(1)}, bf16[64,80,128]{2,1,0:T(8,128)(2,1)}, u32[]{:S(2)}) copy-start(bf16[64,80,128]{2,1,0:T(8,128)(2,1)} %param.3) | copy-start | bytes 3932164
  1.3 0.8 %copy-start.1 = (bf16[2,128,128]{2,1,0:T(8,128)(2,1)S(1)}, bf16[2,128,128]{2,1,0:T(8,128)(2,1)}, u32[]{:S(2)}) copy-start(bf16[2,128,128]{2,1,0:T(8,128)(2,1)} %constant.2.clone.lag_ref) | copy-start | bytes 196612
  2.2 0.7 %copy-start.2 = (s32[80]{0:T(128)S(1)}, s32[80]{0:T(128)}, u32[]{:S(2)}) copy-start(s32[80]{0:T(128)} %mask_ref.1) | copy-start | bytes 964

commit v2 on v1

--- a/solution.py
+++ b/solution.py
@@ -20,7 +20,10 @@
 GROUPS = 4
 ROWS = 112
 DOWN, UP = 0, 1
-DIRECTION = (DOWN, DOWN, DOWN, DOWN)
+DIRECTION = (DOWN, UP, DOWN, DOWN)
+CHUNK = 16
+NEAR_FIRST = (1, 2, 3, 6, 7, 4, 5)
+FAR_FIRST = (4, 5, 6, 7, 2, 3, 1)
 
 
 def lag_tables(windows_all):
@@ -49,12 +52,24 @@
     return (plane * 2 + slot // 4, slot % 4)
 
 
-def kernel(x_ref, mask_ref, lag_ref, out_ref, xf, tf, sent, own, other, made, got, gotf,
-           send_a, recv_a, send_z, recv_z, send_r, recv_r, local):
+def kernel(x_hbm, mask_hbm, lag_hbm, out_ref, x_ref, mask_ref, lag_ref, xf, tf, sent, own, other, made, got, gotf,
+           send_a, recv_a, send_z, recv_z, send_r, recv_r, local, load):
     plane = lax.axis_index("chan") // 2
     quarter = lax.axis_index("tm")
     slot = (lax.axis_index("chan") % 2) * 4 + quarter
     any_up = UP in DIRECTION
+
+    def fetch(n):
+        part = (slice(None), pl.ds(pl.multiple_of(n * CHUNK, CHUNK), CHUNK), slice(None))
+        return pltpu.make_async_copy(x_hbm.at[part], x_ref.at[part], load.at[n])
+
+    chunks = CH // CHUNK
+    fetch_mask = pltpu.make_async_copy(mask_hbm, mask_ref, load.at[chunks])
+    fetch_lag = pltpu.make_async_copy(lag_hbm, lag_ref, load.at[chunks + 1])
+    fetch_mask.start()
+    for n in range(chunks):
+        fetch(n).start()
+    fetch_lag.start()
 
     barrier = pltpu.get_barrier_semaphore()
     greeted = [device(plane, flip(slot, k)) for k in range(1, SLOTS)]
@@ -66,16 +81,11 @@
     lane = lax.broadcasted_iota(jnp.int32, (64, LANES), 1)
     low = lane < 64
 
-    def widen(n, carry):
-        rows = pl.ds(pl.multiple_of(n * 128, 128), 128)
-        xf[rows, :] = x_ref[rows, :].astype(F32)
-        return carry
-
-    lax.fori_loop(0, WIN * CH // 128, widen, 0)
-
-    def turn(channel, place):
+    def turn(channel):
+        t, m = channel // 20, channel % 20
+        place = 16 * t + m + (m // 16) * (48 - 12 * t)
         pair = [xf[pl.ds(channel + k, WIN, stride=CH), :] for k in range(2)]
-        z = jnp.concatenate(pair, axis=0).T
+        z = jnp.concatenate(pair, axis=0).astype(BF16).T.astype(F32)
         power = jnp.sum(z * z, axis=0, keepdims=True) * (1.0 / LANES)
         live0 = mask_ref[channel].astype(F32)
         live1 = mask_ref[channel + 1].astype(F32)
@@ -84,16 +94,23 @@
         tf[pl.ds(place, 64, stride=CH), :] = jnp.where(low, top, pltpu.roll(bottom, 64, 1))
         tf[pl.ds(place + 1, 64, stride=CH), :] = jnp.where(low, pltpu.roll(top, 64, 1), bottom)
 
-    def turn_first(n, carry):
-        turn(20 * (n // 8) + 2 * (n % 8), 2 * n)
+    def prepare(n, carry):
+        fetch(n).wait()
+        first = pl.multiple_of(n * CHUNK, CHUNK)
+
+        def widen(w, c):
+            for k in range(8):
+                row = pl.multiple_of((w * 8 + k) * CH + first, CHUNK)
+                xf[pl.ds(row, CHUNK), :] = x_ref[w * 8 + k, pl.ds(first, CHUNK), :].astype(F32)
+            return c
+
+        lax.fori_loop(0, WIN // 8, widen, 0)
+        for k in range(0, CHUNK, 2):
+            turn(first + k)
         return carry
 
-    def turn_rest(n, carry):
-        turn(20 * (n // 2) + 16 + 2 * (n % 2), 64 + 2 * n)
-        return carry
-
-    lax.fori_loop(0, 32, turn_first, 0)
-    lax.fori_loop(0, 8, turn_rest, 0)
+    fetch_mask.wait()
+    lax.fori_loop(0, chunks, prepare, 0)
 
     def exchange(g, k):
         peer = flip(slot, k)
@@ -105,6 +122,14 @@
     def keep(g):
         return pltpu.make_async_copy(sent.at[slot, g], own.at[g, slot], local.at[g])
 
+    def forward(g, k):
+        step = -1 if DIRECTION[g] == DOWN else 1
+        source = flip(slot, k)
+        return pltpu.make_async_remote_copy(
+            src_ref=own.at[g, source] if k else sent.at[slot, g], dst_ref=other.at[g, source],
+            send_sem=send_z.at[g, k], recv_sem=recv_z.at[g, k],
+            device_id=device(plane + step, slot), device_id_type=MESH)
+
     for g in range(GROUPS):
         def narrow(d, carry, g=g):
             for ff in range(2):
@@ -115,21 +140,10 @@
         lax.fori_loop(0, SLOTS, narrow, 0)
         if g == 0:
             pl.semaphore_wait(barrier, len(greeted))
-        for k in (4, 5, 6, 7, 2, 3, 1):
+        for k in FAR_FIRST:
             exchange(g, k).start()
+        forward(g, 0).start()
         keep(g).start()
-
-    def forward(g):
-        step = -1 if DIRECTION[g] == DOWN else 1
-        return pltpu.make_async_remote_copy(
-            src_ref=own.at[g], dst_ref=other.at[g], send_sem=send_z.at[g], recv_sem=recv_z.at[g],
-            device_id=device(plane + step, slot), device_id_type=MESH)
-
-    for g in range(GROUPS):
-        keep(g).wait()
-        for k in range(1, SLOTS):
-            exchange(g, k).wait_recv()
-        forward(g).start()
 
     sign = jnp.where(low[:1], 1.0, -1.0).astype(F32)
     piece = lax.broadcasted_iota(jnp.int32, (CH, LANES), 1) // 32
@@ -180,13 +194,29 @@
     def retain(g):
         return pltpu.make_async_copy(made.at[g, slot], got.at[g, slot], local.at[GROUPS + g])
 
-    for g in range(GROUPS):
-        forward(g).wait_recv()
+    def pass_on(g):
+        for k in NEAR_FIRST:
+            exchange(g, k).wait_recv()
+            forward(g, k).start()
+
+    def work(g):
+        keep(g).wait()
+        for k in range(SLOTS):
+            forward(g, k).wait_recv()
         cross(g)
         if DIRECTION[g] == DOWN:
             retain(g).start()
-        for k in (4, 5, 6, 7, 2, 3, 1) + ((0,) if DIRECTION[g] == UP else ()):
+        for k in FAR_FIRST + ((0,) if DIRECTION[g] == UP else ()):
             deliver(g, k).start()
+
+    pass_on(0)
+    pass_on(1)
+    pass_on(2)
+    work(0)
+    pass_on(3)
+    work(1)
+    work(2)
+    work(3)
 
     for g in range(GROUPS):
         if DIRECTION[g] == DOWN:
@@ -201,6 +231,7 @@
 
         lax.fori_loop(0, SLOTS, spread, 0)
 
+    fetch_lag.wait()
     sources = GROUPS * SLOTS
     low16 = lax.broadcasted_iota(jnp.int32, (16, LANES), 1) // 32
 
@@ -253,7 +284,8 @@
     for g in range(GROUPS):
         for k in range(1, SLOTS):
             exchange(g, k).wait_send()
-        forward(g).wait_send()
+        for k in range(SLOTS):
+            forward(g, k).wait_send()
         for k in range(0 if DIRECTION[g] == UP else 1, SLOTS):
             deliver(g, k).wait_send()
 
@@ -266,9 +298,12 @@
     return pl.pallas_call(
         kernel,
         out_shape=jax.ShapeDtypeStruct((2, 20, CH, LANES), BF16),
-        in_specs=[vmem, pl.BlockSpec(memory_space=pltpu.SMEM), vmem],
+        in_specs=[pl.BlockSpec(memory_space=pltpu.HBM)] * 3,
         out_specs=vmem,
         scratch_shapes=[
+            pltpu.VMEM((WIN, CH, LANES), BF16),
+            pltpu.SMEM((CH,), jnp.int32),
+            pltpu.VMEM((2, LANES, LANES), BF16),
             pltpu.VMEM((WIN * CH, LANES), F32),
             pltpu.VMEM((64 * CH, LANES), F32),
             pltpu.VMEM((SLOTS, GROUPS, 2, CH, LANES), BF16),
@@ -278,14 +313,14 @@
             pltpu.VMEM((GROUPS, SLOTS, ROWS, LANES), BF16),
             pltpu.VMEM((GROUPS * SLOTS * ROWS, LANES), F32),
             dma((GROUPS, SLOTS)), dma((GROUPS, SLOTS)),
-            dma((GROUPS,)), dma((GROUPS,)),
             dma((GROUPS, SLOTS)), dma((GROUPS, SLOTS)),
-            dma((2 * GROUPS,)),
+            dma((GROUPS, SLOTS)), dma((GROUPS, SLOTS)),
+            dma((2 * GROUPS,)), dma((CH // CHUNK + 2,)),
         ],
         compiler_params=pltpu.CompilerParams(
-            collective_id=0, has_side_effects=True, vmem_limit_bytes=40 * 2**20),
+            collective_id=0, has_side_effects=True, vmem_limit_bytes=62 * 2**20),
         name="correlate",
-    )(spectra.reshape(WIN * CH, LANES), live_mask, tables)
+    )(spectra, live_mask, tables)
 
 
 def solution(mesh):

time: 63 us -> 51.4 us (0.82)
  Pallas kernels: 58.7 us -> 49.2 us
  local copies, waits for them, and re-layouts: 3.7 us -> 2.09 us
    pallas_call x1, Pallas kernels: 58.7 us -> 49.2 us  [shards(): pl.pallas_call(kernel, out_shape=jax.ShapeDtypeStruct((2, 20, CH, LANES),...]
    unnamed x7 -> x1, local copies, waits for them, and re-layouts: 3.7 us -> 2.09 us
where the time goes in v2:
time: 51.4 us; the launch traced here: 51.3 us
  Pallas kernels  49.2 us (96%)
  local copies, waits for them, and re-layouts  2.09 us (4%)
    pallas_call x1, Pallas kernels, shards(): pl.pallas_call(kernel, out_shape=jax.ShapeDtypeStruct((2, 20, CH, LANES),...  49.2 us
    unnamed x1, local copies, waits for them, and re-layouts  2.09 us

profile of v2, /device:TPU:1, one launch (start us, length us, event | category | flops | bytes accessed | tf_op | source)
XLA Modules:
  0.0 51.3 jit_solution(8098000864317575971)
XLA Ops:
  0.0 49.2 %correlate.1 = bf16[2,20,80,128]{3,2,1,0:T(8,128)(2,1)} custom-call(bf16[64,80,128]{2,1,0:T(8,128)(2,1)} %x_hbm.1, s32[80]{0:T(128)} %mask_hbm.1, bf16[2,128,128]{2,1,0:T(8,128)(2,1)} %constant.2.clone.lag_hbm), custom_call_target="tpu_custom_call" | custom-call | tf_op jit(solution)/shard_map/correlate/pallas_call | solution.py:298
  49.2 2.1 %copy.5 = bf16[2,20,80,128]{3,2,1,0:T(8,128)(2,1)} copy(bf16[2,20,80,128]{3,2,1,0:T(8,128)(2,1)} %correlate.1) | data formatting | bytes 1638400

commit v3 on v2

--- a/solution.py
+++ b/solution.py
@@ -20,10 +20,10 @@
 GROUPS = 4
 ROWS = 112
 DOWN, UP = 0, 1
-DIRECTION = (DOWN, UP, DOWN, DOWN)
+DIRECTION = (DOWN, DOWN, DOWN, DOWN)
 CHUNK = 16
-NEAR_FIRST = (1, 2, 3, 6, 7, 4, 5)
-FAR_FIRST = (4, 5, 6, 7, 2, 3, 1)
+NEAR_FIRST = (2, 3, 6, 7, 4, 5)
+SEND_ORDER = (1, 4, 5, 6, 7, 2, 3)
 
 
 def lag_tables(windows_all):
@@ -140,7 +140,7 @@
         lax.fori_loop(0, SLOTS, narrow, 0)
         if g == 0:
             pl.semaphore_wait(barrier, len(greeted))
-        for k in FAR_FIRST:
+        for k in SEND_ORDER:
             exchange(g, k).start()
         forward(g, 0).start()
         keep(g).start()
@@ -206,9 +206,12 @@
         cross(g)
         if DIRECTION[g] == DOWN:
             retain(g).start()
-        for k in FAR_FIRST + ((0,) if DIRECTION[g] == UP else ()):
+        for k in SEND_ORDER + ((0,) if DIRECTION[g] == UP else ()):
             deliver(g, k).start()
 
+    for g in range(GROUPS):
+        exchange(g, 1).wait_recv()
+        forward(g, 1).start()
     pass_on(0)
     pass_on(1)
     pass_on(2)
@@ -318,9 +321,9 @@
             dma((2 * GROUPS,)), dma((CH // CHUNK + 2,)),
         ],
         compiler_params=pltpu.CompilerParams(
-            collective_id=0, has_side_effects=True, vmem_limit_bytes=62 * 2**20),
+            collective_id=0, has_side_effects=True, vmem_limit_bytes=40 * 2**20),
         name="correlate",
-    )(spectra, live_mask, tables)
+    )(*(pltpu.with_memory_space_constraint(a, pltpu.HBM) for a in (spectra, live_mask, tables)))
 
 
 def solution(mesh):

time: 51.4 us -> 48 us (0.934)
  Pallas kernels: 49.2 us -> 46.6 us
  local copies, waits for them, and re-layouts: 2.09 us -> 0.89 us
    pallas_call x1, Pallas kernels: 49.2 us -> 46.6 us  [shards(): pl.pallas_call(kernel, out_shape=jax.ShapeDtypeStruct((2, 20, CH, LANES),...]
    unnamed x1, local copies, waits for them, and re-layouts: 2.09 us -> 0.89 us
where the time goes in v3:
time: 48 us; the launch traced here: 47.5 us
  Pallas kernels  46.6 us (97%)
  local copies, waits for them, and re-layouts  0.89 us (2%)
    pallas_call x1, Pallas kernels, shards(): pl.pallas_call(kernel, out_shape=jax.ShapeDtypeStruct((2, 20, CH, LANES),...  46.6 us

profile of v3, /device:TPU:1, one launch (start us, length us, event | category | flops | bytes accessed | tf_op | source)
XLA Modules:
  0.0 47.5 jit_solution(2959432032421489009)
XLA Ops:
  0.0 46.6 %correlate.1 = bf16[2,20,80,128]{3,2,1,0:T(8,128)(2,1)S(1)} custom-call(bf16[64,80,128]{2,1,0:T(8,128)(2,1)} %x_hbm.1, s32[80]{0:T(128)} %mask_hbm.1, bf16[2,128,128]{2,1,0:T(8,128)(2,1)} %constant.2.clone.lag_hbm), custom_call_target="tpu_custom_call" | custom-call | tf_op jit(solution)/shard_map/correlate/pallas_call | solution.py:301
  46.6 0.9 %copy.5 = bf16[2,20,80,128]{3,2,1,0:T(8,128)(2,1)} copy(bf16[2,20,80,128]{3,2,1,0:T(8,128)(2,1)S(1)} %correlate.1) | data formatting | bytes 1638400

commit v4 on v3

--- a/solution.py
+++ b/solution.py
@@ -34,9 +34,15 @@
     scaling = 1.0 / (2.0 * math.sqrt(64 * windows_all))
     parts = np.stack([weight[:, None] * np.cos(phase), -weight[:, None] * np.sin(phase)]) * scaling
     parts = parts.reshape(2, SLOTS, GROUPS, 2, LANES)
-    main = parts.transpose(0, 3, 2, 1, 4).reshape(LANES, LANES)
-    rest = parts.transpose(3, 0, 2, 1, 4).reshape(LANES, LANES)
-    return np.stack([main, rest]).astype(ml_dtypes.bfloat16)
+    tables = []
+    for half in range(2):
+        here = parts[:, :, 2 * half:2 * half + 2]
+        main = here.transpose(0, 3, 2, 1, 4).reshape(2, 1, 32, LANES)
+        rest = here.transpose(3, 0, 2, 1, 4).reshape(4, 1, 16, LANES)
+        main = np.broadcast_to(main, (2, 4, 32, LANES)).reshape(256, LANES)
+        rest = np.broadcast_to(rest, (4, 8, 16, LANES)).reshape(512, LANES)
+        tables.append(np.concatenate([main, rest]))
+    return np.stack(tables).astype(ml_dtypes.bfloat16)
 
 
 def flip(slot, bits):
@@ -52,7 +58,7 @@
     return (plane * 2 + slot // 4, slot % 4)
 
 
-def kernel(x_hbm, mask_hbm, lag_hbm, out_ref, x_ref, mask_ref, lag_ref, xf, tf, sent, own, other, made, got, gotf,
+def kernel(x_hbm, mask_hbm, lag_hbm, out_ref, x_ref, mask_ref, lag_ref, xf, tf, sent, own, other, made, got, gotf, acc,
            send_a, recv_a, send_z, recv_z, send_r, recv_r, local, load):
     plane = lax.axis_index("chan") // 2
     quarter = lax.axis_index("tm")
@@ -214,75 +220,75 @@
         forward(g, 1).start()
     pass_on(0)
     pass_on(1)
+    lane128 = lax.broadcasted_iota(jnp.int32, (64, LANES), 1)
+
+    def collect(g):
+        retain(g).wait()
+        for k in range(1, SLOTS):
+            deliver(g, k).wait_recv()
+
+        def spread(d, carry):
+            row = pl.multiple_of((g * SLOTS + d) * ROWS, 16)
+            gotf[pl.ds(row, ROWS), :] = got[g, d].astype(F32)
+            return carry
+
+        lax.fori_loop(0, SLOTS, spread, 0)
+
+    def lags(half, first, row_main, row_edge, stride_ff, stride_r):
+        def rows_of(row):
+            return gotf[pl.ds(half * 16 * ROWS + row, 16, stride=ROWS), :]
+
+        z = jnp.concatenate([rows_of(row_edge + j) for j in range(4)] + [jnp.zeros((64, LANES), F32)], axis=0).T
+        pieces = []
+        for j in range(4):
+            mine = lane128[:16] // 16 == j
+            for r in range(2):
+                blocks = [z[(ff * 4 + r * 2 + c) * 16:][:16] for ff in range(2) for c in range(2)]
+                pieces.append(jnp.concatenate([jnp.where(mine, p, 0.0) for p in blocks], axis=1))
+        edge = jnp.dot(jnp.concatenate(pieces, axis=0).astype(BF16), lag_ref[half, pl.ds(256, 512), :],
+                       preferred_element_type=F32)
+        for r in range(2):
+            rows = [rows_of(row_main + ff * stride_ff + r * stride_r + j) for j in range(4) for ff in range(2)]
+            z = jnp.concatenate(rows, axis=0).T
+            lhs = []
+            for j in range(4):
+                mine = lane128 // 32 == j
+                lhs.append(jnp.concatenate([jnp.where(mine, z[:64], 0.0), jnp.where(mine, z[64:], 0.0)], axis=1))
+            body = jnp.dot(jnp.concatenate(lhs, axis=0).astype(BF16), lag_ref[half, pl.ds(0, 256), :],
+                           preferred_element_type=F32)
+            for j in range(4):
+                at = (j * 2 + r) * 16
+                pieces = []
+                for t in range(4):
+                    pieces.append(body[j * 64 + t * 16:j * 64 + (t + 1) * 16])
+                    pieces.append(edge[at + t * 4:at + (t + 1) * 4])
+                value = jnp.concatenate(pieces, axis=0)
+                if half == 0:
+                    acc[r, first + j] = value
+                else:
+                    out_ref[r, first + j] = (acc[r, first + j] + value).astype(BF16)
+
+    def transform(half):
+        def lags_first(n, carry):
+            lags(half, 4 * n, 4 * n, 80 + 4 * n, 32, 16)
+            return carry
+
+        lax.fori_loop(0, 4, lags_first, 0)
+        lags(half, 16, 64, 96 + 4 * quarter, 8, 4)
+
     pass_on(2)
     work(0)
     pass_on(3)
     work(1)
     work(2)
+    fetch_lag.wait()
+    collect(0)
+    collect(1)
+    transform(0)
+    collect(2)
     work(3)
-
-    for g in range(GROUPS):
-        if DIRECTION[g] == DOWN:
-            retain(g).wait()
-        for k in range(0 if DIRECTION[g] == UP else 1, SLOTS):
-            deliver(g, k).wait_recv()
-
-        def spread(d, carry, g=g):
-            row = pl.multiple_of((g * SLOTS + d) * ROWS, 16)
-            gotf[pl.ds(row, ROWS), :] = got[g, d].astype(F32)
-            return carry
-
-        lax.fori_loop(0, SLOTS, spread, 0)
-
-    fetch_lag.wait()
-    sources = GROUPS * SLOTS
-    low16 = lax.broadcasted_iota(jnp.int32, (16, LANES), 1) // 32
-
-    def rows_of(row):
-        return gotf[pl.ds(row, sources, stride=ROWS), :]
-
-    def lags(first, row_main, row_edge, stride_ff, stride_r):
-        z = jnp.concatenate([rows_of(row_edge + j) for j in range(4)], axis=0).T
-        pieces = []
-        for j in range(4):
-            for r in range(2):
-                total = None
-                for ff in range(2):
-                    for c in range(2):
-                        at = (ff * 4 + r * 2 + c) * 16
-                        to = ff * 2 + c
-                        moved = z[at:at + 16]
-                        if (to - j) % 4:
-                            moved = pltpu.roll(moved, ((to - j) % 4) * 32, 1)
-                        total = moved if total is None else jnp.where(low16 == to, moved, total)
-                pieces.append(total)
-        edge = jnp.dot(jnp.concatenate(pieces, axis=0).astype(BF16), lag_ref[1], preferred_element_type=F32)
-        for r in range(2):
-            for half in range(2):
-                rows = []
-                for j in (2 * half, 2 * half + 1):
-                    for ff in range(2):
-                        rows.append(rows_of(row_main + ff * stride_ff + r * stride_r + j))
-                z = jnp.concatenate(rows, axis=0).T
-                top, bottom = z[:64], z[64:]
-                lhs = jnp.concatenate([jnp.where(low, top, pltpu.roll(bottom, 64, 1)),
-                                       jnp.where(low, pltpu.roll(top, 64, 1), bottom)], axis=0)
-                body = jnp.dot(lhs.astype(BF16), lag_ref[0], preferred_element_type=F32)
-                for n in range(2):
-                    j = 2 * half + n
-                    at = (j * 2 + r) * 16
-                    pieces = []
-                    for t in range(4):
-                        pieces.append(body[n * 64 + t * 16:n * 64 + (t + 1) * 16])
-                        pieces.append(edge[at + t * 4:at + (t + 1) * 4])
-                    out_ref[r, first + j] = jnp.concatenate(pieces, axis=0).astype(BF16)
-
-    def lags_first(n, carry):
-        lags(4 * n, 4 * n, 80 + 4 * n, 32, 16)
-        return carry
-
-    lax.fori_loop(0, 4, lags_first, 0)
-    lags(16, 64, 96 + 4 * quarter, 8, 4)
+    collect(3)
+    transform(1)
 
     for g in range(GROUPS):
         for k in range(1, SLOTS):
@@ -306,7 +312,7 @@
         scratch_shapes=[
             pltpu.VMEM((WIN, CH, LANES), BF16),
             pltpu.SMEM((CH,), jnp.int32),
-            pltpu.VMEM((2, LANES, LANES), BF16),
+            pltpu.VMEM((2, 768, LANES), BF16),
             pltpu.VMEM((WIN * CH, LANES), F32),
             pltpu.VMEM((64 * CH, LANES), F32),
             pltpu.VMEM((SLOTS, GROUPS, 2, CH, LANES), BF16),
@@ -315,6 +321,7 @@
             pltpu.VMEM((GROUPS, SLOTS, ROWS, LANES), BF16),
             pltpu.VMEM((GROUPS, SLOTS, ROWS, LANES), BF16),
             pltpu.VMEM((GROUPS * SLOTS * ROWS, LANES), F32),
+            pltpu.VMEM((2, 20, CH, LANES), F32),
             dma((GROUPS, SLOTS)), dma((GROUPS, SLOTS)),
             dma((GROUPS, SLOTS)), dma((GROUPS, SLOTS)),
             dma((GROUPS, SLOTS)), dma((GROUPS, SLOTS)),

time: 48 us -> 48.7 us (1.015)
  Pallas kernels: 46.6 us -> 47.7 us
    pallas_call x1, Pallas kernels: 46.6 us -> 47.7 us  [shards(): pl.pallas_call(kernel, out_shape=jax.ShapeDtypeStruct((2, 20, CH, LANES),...]
where the time goes in v4:
time: 48.7 us; the launch traced here: 48.6 us
  Pallas kernels  47.7 us (98%)
  local copies, waits for them, and re-layouts  0.89 us (2%)
    pallas_call x1, Pallas kernels, shards(): pl.pallas_call(kernel, out_shape=jax.ShapeDtypeStruct((2, 20, CH, LANES),...  47.7 us

profile of v4, /device:TPU:1, one launch (start us, length us, event | category | flops | bytes accessed | tf_op | source)
XLA Modules:
  0.0 48.6 jit_solution(18403257797696179345)
XLA Ops:
  0.0 47.7 %correlate.1 = bf16[2,20,80,128]{3,2,1,0:T(8,128)(2,1)S(1)} custom-call(bf16[64,80,128]{2,1,0:T(8,128)(2,1)} %x_hbm.1, s32[80]{0:T(128)} %mask_hbm.1, bf16[2,768,128]{2,1,0:T(8,128)(2,1)} %constant.2.clone.lag_hbm), custom_call_target="tpu_custom_call" | custom-call | tf_op jit(solution)/shard_map/correlate/pallas_call | solution.py:307
  47.7 0.9 %copy.5 = bf16[2,20,80,128]{3,2,1,0:T(8,128)(2,1)} copy(bf16[2,20,80,128]{3,2,1,0:T(8,128)(2,1)S(1)} %correlate.1) | data formatting | bytes 1638400

commit v5 on v3

--- a/solution.py
+++ b/solution.py
@@ -214,25 +214,28 @@
         forward(g, 1).start()
     pass_on(0)
     pass_on(1)
+    def collect(g):
+        retain(g).wait()
+        for k in range(1, SLOTS):
+            deliver(g, k).wait_recv()
+
+        def spread(d, carry):
+            row = pl.multiple_of((g * SLOTS + d) * ROWS, 16)
+            gotf[pl.ds(row, ROWS), :] = got[g, d].astype(F32)
+            return carry
+
+        lax.fori_loop(0, SLOTS, spread, 0)
+
     pass_on(2)
     work(0)
     pass_on(3)
     work(1)
     work(2)
+    collect(0)
+    collect(1)
     work(3)
-
-    for g in range(GROUPS):
-        if DIRECTION[g] == DOWN:
-            retain(g).wait()
-        for k in range(0 if DIRECTION[g] == UP else 1, SLOTS):
-            deliver(g, k).wait_recv()
-
-        def spread(d, carry, g=g):
-            row = pl.multiple_of((g * SLOTS + d) * ROWS, 16)
-            gotf[pl.ds(row, ROWS), :] = got[g, d].astype(F32)
-            return carry
-
-        lax.fori_loop(0, SLOTS, spread, 0)
+    collect(2)
+    collect(3)
 
     fetch_lag.wait()
     sources = GROUPS * SLOTS
@@ -281,7 +284,7 @@
         lags(4 * n, 4 * n, 80 + 4 * n, 32, 16)
         return carry
 
-    lax.fori_loop(0, 4, lags_first, 0)
+    lax.fori_loop(0, 4, lags_first, 0, unroll=4)
     lags(16, 64, 96 + 4 * quarter, 8, 4)
 
     for g in range(GROUPS):

time: 48 us -> 46.9 us (0.977)
  Pallas kernels: 46.6 us -> 45.5 us
    pallas_call x1, Pallas kernels: 46.6 us -> 45.5 us  [shards(): pl.pallas_call(kernel, out_shape=jax.ShapeDtypeStruct((2, 20, CH, LANES),...]
where the time goes in v5:
time: 46.9 us; the launch traced here: 46.4 us
  Pallas kernels  45.5 us (97%)
  local copies, waits for them, and re-layouts  0.89 us (2%)
    pallas_call x1, Pallas kernels, shards(): pl.pallas_call(kernel, out_shape=jax.ShapeDtypeStruct((2, 20, CH, LANES),...  45.5 us

profile of v5, /device:TPU:1, one launch (start us, length us, event | category | flops | bytes accessed | tf_op | source)
XLA Modules:
  0.0 46.4 jit_solution(4330600762161637499)
XLA Ops:
  0.0 45.5 %correlate.1 = bf16[2,20,80,128]{3,2,1,0:T(8,128)(2,1)S(1)} custom-call(bf16[64,80,128]{2,1,0:T(8,128)(2,1)} %x_hbm.1, s32[80]{0:T(128)} %mask_hbm.1, bf16[2,128,128]{2,1,0:T(8,128)(2,1)} %constant.2.clone.lag_hbm), custom_call_target="tpu_custom_call" | custom-call | tf_op jit(solution)/shard_map/correlate/pallas_call | solution.py:304
  45.5 0.9 %copy.5 = bf16[2,20,80,128]{3,2,1,0:T(8,128)(2,1)} copy(bf16[2,20,80,128]{3,2,1,0:T(8,128)(2,1)S(1)} %correlate.1) | data formatting | bytes 1638400

commit v6 on v5

--- a/solution.py
+++ b/solution.py
@@ -104,7 +104,7 @@
                 xf[pl.ds(row, CHUNK), :] = x_ref[w * 8 + k, pl.ds(first, CHUNK), :].astype(F32)
             return c
 
-        lax.fori_loop(0, WIN // 8, widen, 0)
+        lax.fori_loop(0, WIN // 8, widen, 0, unroll=4)
         for k in range(0, CHUNK, 2):
             turn(first + k)
         return carry
@@ -137,7 +137,7 @@
                 sent[d, g, ff] = tf[pl.ds(row, CH), :].astype(BF16)
             return carry
 
-        lax.fori_loop(0, SLOTS, narrow, 0)
+        lax.fori_loop(0, SLOTS, narrow, 0, unroll=4)
         if g == 0:
             pl.semaphore_wait(barrier, len(greeted))
         for k in SEND_ORDER:
@@ -224,7 +224,7 @@
             gotf[pl.ds(row, ROWS), :] = got[g, d].astype(F32)
             return carry
 
-        lax.fori_loop(0, SLOTS, spread, 0)
+        lax.fori_loop(0, SLOTS, spread, 0, unroll=4)
 
     pass_on(2)
     work(0)

time: 46.9 us -> 46.7 us (level)
  no operation moved by 1% of the time
where the time goes in v6:
time: 46.7 us; the launch traced here: 46.2 us
  Pallas kernels  45.3 us (97%)
  local copies, waits for them, and re-layouts  0.89 us (2%)
    pallas_call x1, Pallas kernels, shards(): pl.pallas_call(kernel, out_shape=jax.ShapeDtypeStruct((2, 20, CH, LANES),...  45.3 us

profile of v6, /device:TPU:1, one launch (start us, length us, event | category | flops | bytes accessed | tf_op | source)
XLA Modules:
  0.0 46.2 jit_solution(2084682902288175635)
XLA Ops:
  0.0 45.3 %correlate.1 = bf16[2,20,80,128]{3,2,1,0:T(8,128)(2,1)S(1)} custom-call(bf16[64,80,128]{2,1,0:T(8,128)(2,1)} %x_hbm.1, s32[80]{0:T(128)} %mask_hbm.1, bf16[2,128,128]{2,1,0:T(8,128)(2,1)} %constant.2.clone.lag_hbm), custom_call_target="tpu_custom_call" | custom-call | tf_op jit(solution)/shard_map/correlate/pallas_call | solution.py:304
  45.3 0.9 %copy.5 = bf16[2,20,80,128]{3,2,1,0:T(8,128)(2,1)} copy(bf16[2,20,80,128]{3,2,1,0:T(8,128)(2,1)S(1)} %correlate.1) | data formatting | bytes 1638400
